TPU v7x, 32 devices: a whole 2x2x4 slice. The times are simulated.
32 devices in a mesh: parts: 2 (over y), inst: 2 (over core), mesh: 8 (over z, x).
Axes of the slice: x: 2, y: 2, z: 4, core: 2. Of those that a mesh axis runs over, the one named last changes fastest.
Arguments:
- state: float32 [16, 4, 2, 64, 256], P(('parts', 'inst'), None, None, 'mesh'), parts along dimension 0, may hold values from -0.5 to 3, as said below
- donor_rows: int32 [8, 2, 2, 64], P('inst', None, None, 'mesh'), may hold values from 0 to 63, as said below
- donor_weights: float32 [8, 2, 2, 64], P('inst', None, None, 'mesh'), may hold values from 0.2 to 0.8, as said below
Outputs:
- state_next: float32 [16, 4, 2, 64, 256], P(('parts', 'inst'), None, None, 'mesh'), parts along dimension 0
- residual: float32 [16, 4, 2, 64, 256], P(('parts', 'inst'), None, None, 'mesh'), parts along dimension 0
There are 2 independent parts, one for each index of `parts`. A program takes and returns all parts, laid end to end along the dimension named above; an argument that names none is the same for every part. Nothing has to cross between parts.
Inputs may be any that keep to these rules, and one draw needn't show every extreme that they name: `state`: density lies in 0.8 to 1.2, both momenta in -0.5 to 0.5, total energy in 2 to 3. For each instance t and side s there is one offset k with donor_rows[t, s, 0, r] = (r + k) mod 64 and donor_rows[t, s, 1, r] = (r + k + 1) mod 64 for every row r. donor_weights[t, s, 1, r] = 1 - donor_weights[t, s, 0, r].
All inputs are finite; a program needn't handle non-finite values.
Results may differ from a plain program's by a relative error of at most 0.0003.
Values sent between devices are 32-bit elements; how exact they have to be, the bound alone decides.
A program may use at most 128 MiB of HBM per device.

v0:
```python
import functools
import math

import jax
import jax.numpy as jnp
from jax import lax
from jax.experimental import pallas as pl
from jax.experimental.pallas import tpu as pltpu
from jax.sharding import PartitionSpec as P

heat_ratio = 1.4
second_coef = 0.5
fourth_coef = 1.0 / 32.0
time_step = 0.05
LANES = 128
MESH = pl.DeviceIdType.MESH


def spectral(offset, total):
    if offset % total == 0:
        return 0.0
    angle = math.pi * offset / total
    return 0.5 * (1.0 - 2.0 * (offset % 2)) * math.cos(angle) / math.sin(angle)


def primitives(value):
    density, axial, circ, energy = value
    inverse = 1.0 / density
    speed_one = axial * inverse
    speed_two = circ * inverse
    pressure = (heat_ratio - 1.0) * (energy - 0.5 * (axial * speed_one + circ * speed_two))
    sound = jnp.sqrt(heat_ratio * pressure * inverse)
    return pressure, sound, speed_one, speed_two


def flux(value, pressure, speed, normal):
    density, axial, circ, energy = value
    return [
        axial if normal == 1 else circ,
        axial * speed + pressure if normal == 1 else axial * speed,
        circ * speed + pressure if normal == 2 else circ * speed,
        (energy + pressure) * speed,
    ]


def face(cells, pressures, radii, fluxes):
    first, second, third, fourth = pressures
    sensor_one = jnp.abs(third - 2.0 * second + first) / (third + 2.0 * second + first)
    sensor_two = jnp.abs(fourth - 2.0 * third + second) / (fourth + 2.0 * third + second)
    eps_two = second_coef * jnp.maximum(sensor_one, sensor_two)
    eps_four = jnp.maximum(0.0, fourth_coef - eps_two)
    radius = 0.5 * (radii[0] + radii[1])
    two = radius * eps_two
    four = radius * eps_four
    out = []
    for c in range(4):
        step = cells[2][c] - cells[1][c]
        third_diff = cells[3][c] - cells[0][c] - 3.0 * step
        out.append(0.5 * (fluxes[0][c] + fluxes[1][c]) - two * step + four * third_diff)
    return out


def lane_roll(value, shift):
    shift = shift % LANES
    return value if shift == 0 else pltpu.roll(value, shift, 1)


def kernel(
    n, local, surfaces, state_ref, rows_ref, weights_ref, next_ref, res_ref,
    field, other, packed_one, packed_two, prims, acc, ghost, send_sem, recv_sem,
):
    me = lax.axis_index("mesh")
    inst = lax.axis_index("inst")
    partner = 1 - inst
    rows = state_ref.shape[3]
    packed = (packed_one, packed_two)
    lane = lax.broadcasted_iota(jnp.int32, (8, LANES), 1)
    sub = lax.broadcasted_iota(jnp.int32, (8, LANES), 0)
    wide_sub = lax.broadcasted_iota(jnp.int32, (8, 2 * LANES), 0)

    barrier = pltpu.get_barrier_semaphore()

    def greet(k, carry):
        pl.semaphore_signal(
            barrier, inc=1, device_id={"mesh": lax.rem(me + k, n)}, device_id_type=MESH
        )
        return carry

    pl.semaphore_signal(barrier, inc=1, device_id={"inst": partner}, device_id_type=MESH)
    lax.fori_loop(1, n, greet, 0)

    for c in range(4):
        block = jnp.stack([state_ref[t, c, s] for t in range(local) for s in range(surfaces)])
        field[0, c, 2 : 2 + rows] = jnp.swapaxes(block, 0, 1)

    place = lane % 4
    lane_row = lane // 16
    weight = []
    for point in range(2):
        total = jnp.zeros((8, LANES), jnp.float32)
        for t in range(local):
            for side in range(2):
                mine = jnp.zeros((8, LANES), jnp.float32)
                for r in range(rows):
                    mine = jnp.where(lane_row == r, weights_ref[t, side, point, r], mine)
                inside = (sub // surfaces == t) & ((place >= 2) if side == 0 else (place < 2))
                total = jnp.where(inside, mine, total)
        weight.append(total)

    def coefficients(offsets):
        out = jnp.zeros((8, 2 * LANES), jnp.float32)
        for t in range(local):
            out = jnp.where(wide_sub // surfaces == t, spectral(offsets[t], 2 * local), out)
        return out

    own_coef = [
        coefficients([t - (t - k) % local for t in range(local)]) for k in range(local)
    ]
    other_coef = [
        coefficients([local + t - (t - k) % local for t in range(local)]) for k in range(local)
    ]

    def pack(section):
        total = jnp.zeros((8, LANES), jnp.float32)
        for r in range(rows):
            for c in range(4):
                rotor = field[section, c, 2 + r, :, 0:LANES]
                stator = field[section, c, 2 + r, :, LANES : 2 * LANES]
                edge = jnp.where(lane < 2, stator, rotor)
                block = r * 4 + c
                total = jnp.where(lane // 4 == block, lane_roll(edge, block * 4 + 2), total)
        packed[section][me] = total

    def copies(section):
        down = lax.rem(me + n - 1, n)
        up = lax.rem(me + 1, n)
        top = pltpu.make_async_remote_copy(
            field.at[section, :, rows : rows + 2], field.at[section, :, 0:2],
            send_sem.at[section, 0], recv_sem.at[section, 0],
            device_id={"mesh": up}, device_id_type=MESH,
        )
        bottom = pltpu.make_async_remote_copy(
            field.at[section, :, 2:4], field.at[section, :, rows + 2 : rows + 4],
            send_sem.at[section, 1], recv_sem.at[section, 1],
            device_id={"mesh": down}, device_id_type=MESH,
        )
        cross = pltpu.make_async_remote_copy(
            field.at[section, :, 2 : 2 + rows], other.at[section],
            send_sem.at[section, 2], recv_sem.at[section, 2],
            device_id={"inst": partner}, device_id_type=MESH,
        )
        return top, bottom, cross

    def send_columns(section):
        def one(k, carry):
            pltpu.make_async_remote_copy(
                packed[section].at[me], packed[section].at[me],
                send_sem.at[section, 3], recv_sem.at[section, 3],
                device_id={"mesh": lax.rem(me + k, n)}, device_id_type=MESH,
            ).start()
            return carry

        lax.fori_loop(1, n, one, 0)

    def all_columns(section):
        return pltpu.make_async_remote_copy(
            packed[section].at[0 : n - 1], packed[section].at[0 : n - 1],
            send_sem.at[section, 3], recv_sem.at[section, 3],
            device_id={"inst": partner}, device_id_type=MESH,
        )

    def interpolate(section):
        donors = [jnp.zeros((8, LANES), jnp.float32)] * 2
        for t in range(local):
            for side in range(2):
                start = rows_ref[t, side, 0, 0]
                block = start // rows
                offset = start - block * rows
                low = packed[section][block]
                high = packed[section][lax.rem(block + 1, n)]
                inside = (sub // surfaces == t) & ((place >= 2) if side == 0 else (place < 2))
                for point in range(2):
                    shift = (offset + point) * 16
                    picked = jnp.where(lane >= shift, low, high)
                    picked = pltpu.roll(picked, lax.rem(LANES - shift, LANES), 1)
                    donors[point] = jnp.where(inside, picked, donors[point])
        total = weight[0] * donors[0] + weight[1] * donors[1]
        for r in range(rows):
            for c in range(4):
                ghost[r, c] = lane_roll(total, -(r * 4 + c) * 4 - 2)

    def store_primitives(section, row):
        value = [field[section, c, row] for c in range(4)]
        for i, item in enumerate(primitives(value)):
            prims[i, row] = item

    def circ_face(section, row):
        cells = [[field[section, c, row + k] for c in range(4)] for k in (-1, 0, 1, 2)]
        pressures = [prims[0, row + k] for k in (-1, 0, 1, 2)]
        speeds = [prims[3, row + k] for k in (0, 1)]
        radii = [jnp.abs(speeds[k]) + prims[1, row + k] for k in (0, 1)]
        fluxes = [flux(cells[1 + k], pressures[1 + k], speeds[k], 2) for k in (0, 1)]
        return face(cells, pressures, radii, fluxes)

    def axial_term(section, row):
        sides = [
            [field[section, c, row + 2, :, h * LANES : (h + 1) * LANES] for c in range(4)]
            for h in range(2)
        ]
        west, east, ends = [[], []], [[], []], []
        for c in range(4):
            interp = ghost[row, c]
            first = jnp.broadcast_to(sides[0][c][:, 0:1], (8, LANES))
            final = jnp.broadcast_to(sides[1][c][:, LANES - 1 : LANES], (8, LANES))
            low = lane < 64
            west[0].append(jnp.where(low, sides[0][c], first))
            west[1].append(jnp.where(low, sides[1][c], interp))
            east[0].append(jnp.where(low, interp, sides[0][c]))
            east[1].append(jnp.where(low, final, sides[1][c]))
            window = west[0][c]
            for source, shift in ((east[0][c], 32), (west[1][c], 64), (east[1][c], 96)):
                inside = (lane >= shift - 16) & (lane < shift + 16)
                window = jnp.where(inside, lane_roll(source, shift), window)
            ends.append(window)
        end_pressure, end_sound, end_speed, _ = primitives(ends)
        end_radius = jnp.abs(end_speed) + end_sound
        end_flux = flux(ends, end_pressure, end_speed, 1)

        def moved(value, shift):
            return [lane_roll(v, shift) for v in value]

        end_face = face(
            [moved(ends, 1), ends, moved(ends, -1), moved(ends, -2)],
            [lane_roll(end_pressure, s) for s in (1, 0, -1, -2)],
            [end_radius, lane_roll(end_radius, -1)],
            [end_flux, moved(end_flux, -1)],
        )
        out = []
        for h in range(2):
            cut = slice(h * LANES, (h + 1) * LANES)
            value = sides[h]
            pressure = prims[0, row + 2, :, cut]
            sound = prims[1, row + 2, :, cut]
            speed = prims[2, row + 2, :, cut]
            radius = jnp.abs(speed) + sound
            flow = flux(value, pressure, speed, 1)
            shift_west, shift_east = 64 * h, 32 + 64 * h
            before_p = lane_roll(end_pressure, -shift_west)
            after_p = lane_roll(end_pressure, -shift_east)

            def previous(own, edge):
                return lane_roll(jnp.where(lane == LANES - 1, edge, own), 1)

            def second_next(own, edge):
                return lane_roll(jnp.where(lane == 0, edge, own), -2)

            main = face(
                [
                    [previous(value[c], west[h][c]) for c in range(4)],
                    value,
                    moved(value, -1),
                    [second_next(value[c], east[h][c]) for c in range(4)],
                ],
                [
                    previous(pressure, before_p),
                    pressure,
                    lane_roll(pressure, -1),
                    second_next(pressure, after_p),
                ],
                [radius, lane_roll(radius, -1)],
                [flow, moved(flow, -1)],
            )
            part = []
            for c in range(4):
                right = jnp.where(lane == LANES - 1, lane_roll(end_face[c], -shift_east), main[c])
                left = previous(main[c], lane_roll(end_face[c], -shift_west))
                part.append(right - left)
            out.append(part)
        return [jnp.concatenate([out[0][c], out[1][c]], axis=1) for c in range(4)]

    def own_part(section, row):
        store_primitives(section, row + 2)
        for c in range(4):
            value = field[section, c, row + 2]
            total = own_coef[1] * pltpu.roll(value, surfaces, 0)
            for k in range(2, local):
                total += own_coef[k] * pltpu.roll(value, surfaces * k, 0)
            acc[c, row] = total

    def run(section):
        top, bottom, cross = copies(section)
        top.start()
        bottom.start()
        pack(section)
        send_columns(section)
        cross.start()

        def prepare(row, carry):
            own_part(section, row)
            return carry

        lax.fori_loop(0, rows, prepare, 0)
        cross.wait_recv()

        def others(row, carry):
            for c in range(4):
                value = other[section, c, row]
                total = acc[c, row] + other_coef[0] * value
                for k in range(1, local):
                    total += other_coef[k] * pltpu.roll(value, surfaces * k, 0)
                acc[c, row] = total
            return carry

        lax.fori_loop(0, rows, others, 0)
        all_columns(section).wait_recv()
        interpolate(section)

        def axial(row, carry):
            term = axial_term(section, row)
            for c in range(4):
                acc[c, row] += term[c]
            return carry

        lax.fori_loop(0, rows, axial, 0)
        top.wait_recv()
        bottom.wait_recv()
        for row in (0, 1, rows + 2, rows + 3):
            store_primitives(section, row)

        def circ(row, left):
            right = circ_face(section, row + 2)
            for c in range(4):
                total = acc[c, row] + (right[c] - left[c])
                if section == 0:
                    field[1, c, row + 2] = field[0, c, row + 2] - 0.5 * time_step * total
                else:
                    acc[c, row] = total
            return right

        lax.fori_loop(0, rows, circ, circ_face(section, 1))

    pl.semaphore_wait(barrier, n)
    run(0)
    run(1)
    for c in range(4):
        block = jnp.swapaxes(acc[c], 0, 1)
        for t in range(local):
            for s in range(surfaces):
                value = block[t * surfaces + s]
                res_ref[t, c, s] = value
                next_ref[t, c, s] = state_ref[t, c, s] - time_step * value
    for section in range(2):
        for copy in copies(section):
            copy.wait_send()
        all_columns(section).wait_send()


def per_device(n, state, donor_rows, donor_weights):
    local, _, surfaces, rows, columns = state.shape
    shape = jax.ShapeDtypeStruct(state.shape, jnp.float32)
    vmem = pl.BlockSpec(memory_space=pltpu.VMEM)
    smem = pl.BlockSpec(memory_space=pltpu.SMEM)
    return tuple(
        pl.pallas_call(
            functools.partial(kernel, n, local, surfaces),
            out_shape=[shape, shape],
            in_specs=[vmem, smem, smem],
            out_specs=[vmem, vmem],
            scratch_shapes=[
                pltpu.VMEM((2, 4, rows + 4, 8, columns), jnp.float32),
                pltpu.VMEM((2, 4, rows, 8, columns), jnp.float32),
                pltpu.VMEM((n, 8, LANES), jnp.float32),
                pltpu.VMEM((n, 8, LANES), jnp.float32),
                pltpu.VMEM((4, rows + 4, 8, columns), jnp.float32),
                pltpu.VMEM((4, rows, 8, columns), jnp.float32),
                pltpu.VMEM((rows, 4, 8, LANES), jnp.float32),
                pltpu.SemaphoreType.DMA((2, 4)),
                pltpu.SemaphoreType.DMA((2, 4)),
            ],
            compiler_params=pltpu.CompilerParams(
                collective_id=0, has_side_effects=True, vmem_limit_bytes=24 * 2**20
            ),
        )(state, donor_rows, donor_weights)
    )


def solution(mesh):
    return jax.shard_map(
        functools.partial(per_device, mesh.shape["mesh"]),
        mesh=mesh,
        in_specs=(
            P(("parts", "inst"), None, None, "mesh", None),
            P("inst", None, None, "mesh"),
            P("inst", None, None, "mesh"),
        ),
        out_specs=(
            P(("parts", "inst"), None, None, "mesh", None),
            P(("parts", "inst"), None, None, "mesh", None),
        ),
        check_vma=False,
    )
```

profile of v0, /device:TPU:0, one launch (start us, length us, event | category | flops | bytes accessed | tf_op | source)
XLA Modules:
  0.0 28.2 jit_solution(6792682997423252657)
XLA Ops:
  0.6 0.0 copy-start
  0.6 0.9 %copy-done = f32[4,4,2,8,256]{4,3,2,1,0:T(8,128)S(1)} copy-done((f32[4,4,2,8,256]{4,3,2,1,0:T(8,128)S(1)}, f32[4,4,2,8,256]{4,3,2,1,0:T(8,128)}, u32[]{:S(2)}) %copy-start) | copy-done | bytes 262168
  1.6 0.0 copy-start.1
  1.6 0.7 %copy-done.1 = s32[4,2,2,8]{3,2,1,0:T(2,128)S(1)} copy-done((s32[4,2,2,8]{3,2,1,0:T(2,128)S(1)}, s32[4,2,2,8]{3,2,1,0:T(2,128)}, u32[]{:S(2)}) %copy-start.1) | copy-done | bytes 536
  2.3 0.0 copy-start.2
  2.3 0.7 %copy-done.2 = f32[4,2,2,8]{3,2,1,0:T(2,128)S(1)} copy-done((f32[4,2,2,8]{3,2,1,0:T(2,128)S(1)}, f32[4,2,2,8]{3,2,1,0:T(2,128)}, u32[]{:S(2)}) %copy-start.2) | copy-done | bytes 536
  3.0 23.8 %shard_map.50 = (f32[4,4,2,8,256]{4,3,2,1,0:T(8,128)S(1)}, f32[4,4,2,8,256]{4,3,2,1,0:T(8,128)S(1)}) custom-call(f32[4,4,2,8,256]{4,3,2,1,0:T(8,128)S(1)} %copy-done, s32[4,2,2,8]{3,2,1,0:T(2,128)S(1)} %copy-done.1, f32[4,2,2,8]{3,2,1,0:T(2,128)S(1)} %copy-done.2), custom_call_target="tpu_custom_call" | custom-call | tf_op jit(solution)/shard_map/pallas_call | solution.py:364
  26.8 0.7 %copy.7 = f32[4,4,2,8,256]{4,3,2,1,0:T(8,128)} copy(f32[4,4,2,8,256]{4,3,2,1,0:T(8,128)S(1)} %get-tuple-element.4) | data formatting | bytes 524288
  27.5 0.7 %copy.8 = f32[4,4,2,8,256]{4,3,2,1,0:T(8,128)} copy(f32[4,4,2,8,256]{4,3,2,1,0:T(8,128)S(1)} %get-tuple-element.5) | data formatting | bytes 524288
Async XLA Ops:
  0.6 1.0 %copy-start = (f32[4,4,2,8,256]{4,3,2,1,0:T(8,128)S(1)}, f32[4,4,2,8,256]{4,3,2,1,0:T(8,128)}, u32[]{:S(2)}) copy-start(f32[4,4,2,8,256]{4,3,2,1,0:T(8,128)} %state_ref.1) | copy-start | bytes 786436
  1.6 0.7 %copy-start.1 = (s32[4,2,2,8]{3,2,1,0:T(2,128)S(1)}, s32[4,2,2,8]{3,2,1,0:T(2,128)}, u32[]{:S(2)}) copy-start(s32[4,2,2,8]{3,2,1,0:T(2,128)} %rows_ref.1) | copy-start | bytes 1540
  2.3 0.7 %copy-start.2 = (f32[4,2,2,8]{3,2,1,0:T(2,128)S(1)}, f32[4,2,2,8]{3,2,1,0:T(2,128)}, u32[]{:S(2)}) copy-start(f32[4,2,2,8]{3,2,1,0:T(2,128)} %weights_ref.1) | copy-start | bytes 1540
where the time goes:
time: 28.5 us; the launch traced here: 28.2 us
  Pallas kernels  23.8 us (84%)
  local copies, waits for them, and re-layouts  3.74 us (13%)
  between operations  0.65 us (2%)
    pallas_call x1, Pallas kernels, per_device(): pl.pallas_call(functools.partial(kernel, n, local, surfaces), out_shape=[...  23.8 us
    unnamed x8, local copies, waits for them, and re-layouts  3.74 us

commit v1 on v0

v1 whole, which is shorter than its diff:
```python
import functools
import math

import jax
import jax.numpy as jnp
from jax import lax
from jax.experimental import pallas as pl
from jax.experimental.pallas import tpu as pltpu
from jax.sharding import PartitionSpec as P

heat_ratio = 1.4
second_coef = 0.5
fourth_coef = 1.0 / 32.0
time_step = 0.05
LANES = 128
MESH = pl.DeviceIdType.MESH


def spectral(offset, total):
    if offset % total == 0:
        return 0.0
    angle = math.pi * offset / total
    return 0.5 * (1.0 - 2.0 * (offset % 2)) * math.cos(angle) / math.sin(angle)


def primitives(value):
    density, axial, circ, energy = value
    inverse = 1.0 / density
    speed_one = axial * inverse
    speed_two = circ * inverse
    pressure = (heat_ratio - 1.0) * (energy - 0.5 * (axial * speed_one + circ * speed_two))
    sound = jnp.sqrt(heat_ratio * pressure * inverse)
    return pressure, sound, speed_one, speed_two


def flux(value, pressure, speed, normal):
    density, axial, circ, energy = value
    return [
        axial if normal == 1 else circ,
        axial * speed + pressure if normal == 1 else axial * speed,
        circ * speed + pressure if normal == 2 else circ * speed,
        (energy + pressure) * speed,
    ]


def sensor(before, center, after):
    twice = 2.0 * center
    return jnp.abs(after - twice + before) / (after + twice + before)


def face(cells, sensors, radii, fluxes):
    eps_two = second_coef * jnp.maximum(sensors[0], sensors[1])
    eps_four = jnp.maximum(0.0, fourth_coef - eps_two)
    radius = 0.5 * (radii[0] + radii[1])
    two = radius * eps_two
    four = radius * eps_four
    out = []
    for c in range(4):
        step = cells[2][c] - cells[1][c]
        third_diff = cells[3][c] - cells[0][c] - 3.0 * step
        out.append(0.5 * (fluxes[0][c] + fluxes[1][c]) - two * step + four * third_diff)
    return out


def lane_roll(value, shift):
    shift = shift % LANES
    return value if shift == 0 else pltpu.roll(value, shift, 1)


def kernel(
    n, local, surfaces, state_in, rows_in, weights_in, half_ref,
    state_ref, rows_ref, weights_ref, field, other, packed_one, packed_two, prims, acc, edges,
    local_sem, send_sem, recv_sem,
):
    me = lax.axis_index("mesh")
    inst = lax.axis_index("inst")
    partner = 1 - inst
    rows = state_ref.shape[3]
    packed = (packed_one, packed_two)
    lane = lax.broadcasted_iota(jnp.int32, (8, LANES), 1)
    sub = lax.broadcasted_iota(jnp.int32, (8, LANES), 0)
    wide_sub = lax.broadcasted_iota(jnp.int32, (8, 2 * LANES), 0)

    loads = [
        pltpu.make_async_copy(source, target, local_sem.at[i])
        for i, (source, target) in enumerate(
            ((state_in, state_ref), (rows_in, rows_ref), (weights_in, weights_ref))
        )
    ]
    for load in loads:
        load.start()
    barrier = pltpu.get_barrier_semaphore()

    def greet(k, carry):
        pl.semaphore_signal(
            barrier, inc=1, device_id={"mesh": lax.rem(me + k, n)}, device_id_type=MESH
        )
        return carry

    pl.semaphore_signal(barrier, inc=1, device_id={"inst": partner}, device_id_type=MESH)
    lax.fori_loop(1, n, greet, 0)

    loads[0].wait()
    for c in range(4):
        block = jnp.stack([state_ref[t, c, s] for t in range(local) for s in range(surfaces)])
        field[0, c, 2 : 2 + rows] = jnp.swapaxes(block, 0, 1)

    loads[1].wait()
    loads[2].wait()
    place = lane % 4
    lane_row = lane // 16
    weight = []
    for point in range(2):
        total = jnp.zeros((8, LANES), jnp.float32)
        for t in range(local):
            for side in range(2):
                mine = jnp.zeros((8, LANES), jnp.float32)
                for r in range(rows):
                    mine = jnp.where(lane_row == r, weights_ref[t, side, point, r], mine)
                inside = (sub // surfaces == t) & ((place >= 2) if side == 0 else (place < 2))
                total = jnp.where(inside, mine, total)
        weight.append(total)

    def coefficients(offsets):
        out = jnp.zeros((8, 2 * LANES), jnp.float32)
        for t in range(local):
            out = jnp.where(wide_sub // surfaces == t, spectral(offsets[t], 2 * local), out)
        return out

    own_coef = [None] + [
        coefficients([t - (t - k) % local for t in range(local)]) for k in range(1, local)
    ]
    other_coef = [
        coefficients([local + t - (t - k) % local for t in range(local)]) for k in range(local)
    ]

    spot = lane % 16

    def pack(section):
        out = []
        for c in range(4):
            total = jnp.zeros((8, LANES), jnp.float32)
            for r in range(rows):
                rotor = field[section, c, 2 + r, :, 0:LANES]
                stator = field[section, c, 2 + r, :, LANES : 2 * LANES]
                edge = jnp.where(lane < 64, stator, rotor)
                total = jnp.where(lane_row == r, lane_roll(edge, r * 16 + 3), total)
            edges[section, c] = total
            out.append(total)
        total = lane_roll(out[0], -1)
        for c in range(1, 4):
            total = jnp.where(spot // 4 == c, lane_roll(out[c], c * 4 - 1), total)
        packed[section][me] = total

    def copies(section):
        down = lax.rem(me + n - 1, n)
        up = lax.rem(me + 1, n)
        top = pltpu.make_async_remote_copy(
            field.at[section, :, rows : rows + 2], field.at[section, :, 0:2],
            send_sem.at[section, 0], recv_sem.at[section, 0],
            device_id={"mesh": up}, device_id_type=MESH,
        )
        bottom = pltpu.make_async_remote_copy(
            field.at[section, :, 2:4], field.at[section, :, rows + 2 : rows + 4],
            send_sem.at[section, 1], recv_sem.at[section, 1],
            device_id={"mesh": down}, device_id_type=MESH,
        )
        cross = pltpu.make_async_remote_copy(
            field.at[section, :, 2 : 2 + rows], other.at[section],
            send_sem.at[section, 2], recv_sem.at[section, 2],
            device_id={"inst": partner}, device_id_type=MESH,
        )
        return top, bottom, cross

    def send_columns(section):
        def one(k, carry):
            pltpu.make_async_remote_copy(
                packed[section].at[me], packed[section].at[me],
                send_sem.at[section, 3], recv_sem.at[section, 3],
                device_id={"mesh": lax.rem(me + k, n)}, device_id_type=MESH,
            ).start()
            return carry

        lax.fori_loop(1, n, one, 0)

    def all_columns(section):
        return pltpu.make_async_remote_copy(
            packed[section].at[0 : n - 1], packed[section].at[0 : n - 1],
            send_sem.at[section, 3], recv_sem.at[section, 3],
            device_id={"inst": partner}, device_id_type=MESH,
        )

    def interpolate(section):
        donors = [jnp.zeros((8, LANES), jnp.float32)] * 2
        for t in range(local):
            for side in range(2):
                start = rows_ref[t, side, 0, 0]
                block = start // rows
                offset = start - block * rows
                low = packed[section][block]
                high = packed[section][lax.rem(block + 1, n)]
                inside = (sub // surfaces == t) & ((place >= 2) if side == 0 else (place < 2))
                for point in range(2):
                    shift = (offset + point) * 16
                    picked = jnp.where(lane >= shift, low, high)
                    picked = pltpu.roll(picked, lax.rem(LANES - shift, LANES), 1)
                    donors[point] = jnp.where(inside, picked, donors[point])
        total = weight[0] * donors[0] + weight[1] * donors[1]
        window = []
        for c in range(4):
            near = edges[section, c]
            value = jnp.where(spot < 3, near, lane_roll(near, 7))
            value = jnp.where((spot == 3) | (spot == 4), lane_roll(total, 1 - 4 * c), value)
            value = jnp.where((spot == 8) | (spot == 9), lane_roll(total, 8 - 4 * c), value)
            window.append(jnp.where((spot < 5) | ((spot >= 8) & (spot < 13)), value, near_one[c]))
        pressure, sound, speed, _ = primitives(window)
        radius = jnp.abs(speed) + sound
        flow = flux(window, pressure, speed, 1)
        sense = sensor(lane_roll(pressure, 1), pressure, lane_roll(pressure, -1))
        edge_face = face(
            [moved(window, 1), window, moved(window, -1), moved(window, -2)],
            [sense, lane_roll(sense, -1)],
            [radius, lane_roll(radius, -1)],
            [flow, moved(flow, -1)],
        )
        valid = (spot == 1) | (spot == 2) | (spot == 9) | (spot == 10)
        fix = []
        for c in range(4):
            value = jnp.where(valid, edge_face[c], 0.0)
            value = value - lane_roll(value, 1)
            fix.append(jnp.where(spot < 3, value, lane_roll(value, -7)))
        for c in range(4):
            for r in range(rows):
                moved_back = lane_roll(fix[c], -(r * 16 + 3))
                acc[c, r, :, 0:LANES] += jnp.where(lane >= LANES - 2, moved_back, 0.0)
                acc[c, r, :, LANES : 2 * LANES] += jnp.where(lane < 2, moved_back, 0.0)

    near_one = [1.0, 0.0, 0.0, 2.0]

    def moved(value, shift):
        return [lane_roll(v, shift) for v in value]

    def store_primitives(section, row):
        value = [field[section, c, row] for c in range(4)]
        for i, item in enumerate(primitives(value)):
            prims[i, row] = item

    def row_sensor(row):
        return sensor(prims[0, row - 1], prims[0, row], prims[0, row + 1])

    def circ_face(section, row, before):
        after = row_sensor(row + 1)
        cells = [[field[section, c, row + k] for c in range(4)] for k in (-1, 0, 1, 2)]
        speeds = [prims[3, row + k] for k in (0, 1)]
        radii = [jnp.abs(speeds[k]) + prims[1, row + k] for k in (0, 1)]
        fluxes = [flux(cells[1 + k], prims[0, row + k], speeds[k], 2) for k in (0, 1)]
        return face(cells, [before, after], radii, fluxes), after

    def axial_half(section, row, h):
        cut = slice(h * LANES, (h + 1) * LANES)
        value = [field[section, c, row + 2, :, cut] for c in range(4)]
        pressure = prims[0, row + 2, :, cut]
        speed = prims[2, row + 2, :, cut]
        radius = jnp.abs(speed) + prims[1, row + 2, :, cut]
        flow = flux(value, pressure, speed, 1)
        first, last = lane == 0, lane == LANES - 1

        def before(own):
            return jnp.where(first, own, lane_roll(own, 1)) if h == 0 else lane_roll(own, 1)

        def after(own):
            return jnp.where(last, own, lane_roll(own, -1)) if h == 1 else lane_roll(own, -1)

        following = [after(v) for v in value]
        second = moved(value, -2)
        if h == 1:
            second = [jnp.where(lane >= LANES - 2, a, b) for a, b in zip(following, second)]
        sense = sensor(before(pressure), pressure, after(pressure))
        sense_after = lane_roll(sense, -1)
        if h == 1:
            sense_after = jnp.where(last, 0.0, sense_after)
        right = face(
            [[before(v) for v in value], value, following, second],
            [sense, sense_after],
            [radius, after(radius)],
            [flow, [after(f) for f in flow]],
        )
        keep = lane < LANES - 2 if h == 0 else lane > 0
        right = [jnp.where(keep, f, 0.0) for f in right]
        if h == 0:
            four = radius * jnp.maximum(0.0, fourth_coef - second_coef * sense)
            start = [flow[c] + four * (following[c] - value[c]) for c in range(4)]
        else:
            start = [0.0] * 4
        return [right[c] - jnp.where(first, start[c], lane_roll(right[c], 1)) for c in range(4)]

    def source(values, coefs, total):
        for k, coef in enumerate(coefs):
            if coef is not None:
                value = values if k == 0 else pltpu.roll(values, surfaces * k, 0)
                total = coef * value if total is None else total + coef * value
        return total

    def alone(section):
        def one(row, carry):
            store_primitives(section, row + 2)
            halves = [axial_half(section, row, h) for h in range(2)]
            for c in range(4):
                term = jnp.concatenate([halves[0][c], halves[1][c]], axis=1)
                acc[c, row] = source(field[section, c, row + 2], own_coef, term)
            return carry

        lax.fori_loop(0, rows, one, 0, unroll=2)

    def send(section):
        top, bottom, cross = copies(section)
        top.start()
        bottom.start()
        send_columns(section)
        cross.start()

    def together(section):
        top, bottom, cross = copies(section)
        cross.wait_recv()

        def others(row, carry):
            for c in range(4):
                acc[c, row] = source(other[section, c, row], other_coef, acc[c, row])
            return carry

        lax.fori_loop(0, rows, others, 0, unroll=2)
        all_columns(section).wait_recv()
        interpolate(section)
        top.wait_recv()
        bottom.wait_recv()
        for row in (0, 1, rows + 2, rows + 3):
            store_primitives(section, row)

        def circ(row, carry):
            left, sense = carry
            right, sense = circ_face(section, row + 2, sense)
            for c in range(4):
                total = acc[c, row] + (right[c] - left[c])
                if section == 0:
                    field[1, c, row + 2] = field[0, c, row + 2] - 0.5 * time_step * total
                else:
                    acc[c, row] = 0.5 * total
            return right, sense

        lax.fori_loop(0, rows, circ, circ_face(section, 1, row_sensor(1)))

    pack(0)
    alone(0)
    pl.semaphore_wait(barrier, n)
    send(0)
    together(0)
    pack(1)
    send(1)
    alone(1)
    together(1)
    for c in range(4):
        block = jnp.swapaxes(acc[c], 0, 1)
        for t in range(local):
            for s in range(surfaces):
                half_ref[t, c, s] = block[t * surfaces + s]
    for section in range(2):
        for copy in copies(section):
            copy.wait_send()
        all_columns(section).wait_send()


def per_device(n, state, donor_rows, donor_weights):
    local, _, surfaces, rows, columns = state.shape
    half = pl.pallas_call(
        functools.partial(kernel, n, local, surfaces),
        out_shape=jax.ShapeDtypeStruct(state.shape, jnp.float32),
        in_specs=[pl.BlockSpec(memory_space=pltpu.HBM)] * 3,
        out_specs=pl.BlockSpec(memory_space=pltpu.VMEM),
        scratch_shapes=[
            pltpu.VMEM(state.shape, jnp.float32),
            pltpu.SMEM(donor_rows.shape, jnp.int32),
            pltpu.SMEM(donor_weights.shape, jnp.float32),
            pltpu.VMEM((2, 4, rows + 4, 8, columns), jnp.float32),
            pltpu.VMEM((2, 4, rows, 8, columns), jnp.float32),
            pltpu.VMEM((n, 8, LANES), jnp.float32),
            pltpu.VMEM((n, 8, LANES), jnp.float32),
            pltpu.VMEM((4, rows + 4, 8, columns), jnp.float32),
            pltpu.VMEM((4, rows, 8, columns), jnp.float32),
            pltpu.VMEM((2, 4, 8, LANES), jnp.float32),
            pltpu.SemaphoreType.DMA((3,)),
            pltpu.SemaphoreType.DMA((2, 4)),
            pltpu.SemaphoreType.DMA((2, 4)),
        ],
        compiler_params=pltpu.CompilerParams(
            collective_id=0, has_side_effects=True, vmem_limit_bytes=24 * 2**20
        ),
    )(state, donor_rows, donor_weights)
    return state - (2.0 * time_step) * half, half + half


def solution(mesh):
    return jax.shard_map(
        functools.partial(per_device, mesh.shape["mesh"]),
        mesh=mesh,
        in_specs=(
            P(("parts", "inst"), None, None, "mesh", None),
            P("inst", None, None, "mesh"),
            P("inst", None, None, "mesh"),
        ),
        out_specs=(
            P(("parts", "inst"), None, None, "mesh", None),
            P(("parts", "inst"), None, None, "mesh", None),
        ),
        check_vma=False,
    )
```

time: 28.5 us -> 21.8 us (0.76)
  Pallas kernels: 23.8 us -> 17.8 us
  local copies, waits for them, and re-layouts: 3.74 us -> 2.34 us
  other arithmetic: 0 us -> 0.84 us
    pallas_call x1, Pallas kernels: 23.8 us -> 17.8 us  [per_device(): pl.pallas_call(functools.partial(kernel, n, local, surfaces), out_shape=j...]
    unnamed x8 -> x6, local copies, waits for them, and re-layouts: 3.74 us -> 2.34 us
    sub x0 -> x1, other arithmetic: none -> 0.84 us  [per_device(): return (state - 2.0 * time_step * half, half + half)]
where the time goes in v1:
time: 21.8 us; the launch traced here: 21.6 us
  Pallas kernels  17.8 us (82%)
  local copies, waits for them, and re-layouts  2.34 us (11%)
  other arithmetic  0.84 us (4%)
  between operations  0.65 us (3%)
    pallas_call x1, Pallas kernels, per_device(): pl.pallas_call(functools.partial(kernel, n, local, surfaces), out_shape=j...  17.8 us
    unnamed x6, local copies, waits for them, and re-layouts  2.34 us
    sub x1, other arithmetic, per_device(): return (state - 2.0 * time_step * half, half + half)  0.84 us

profile of v1, /device:TPU:0, one launch (start us, length us, event | category | flops | bytes accessed | tf_op | source)
XLA Modules:
  0.0 21.6 jit_solution(11252181066207162430)
XLA Ops:
  0.6 0.0 copy-start
  0.6 0.9 %copy-done = f32[4,4,2,8,256]{4,3,2,1,0:T(8,128)S(1)} copy-done((f32[4,4,2,8,256]{4,3,2,1,0:T(8,128)S(1)}, f32[4,4,2,8,256]{4,3,2,1,0:T(8,128)}, u32[]{:S(2)}) %copy-start) | copy-done | bytes 262168
  1.6 0.0 copy-start.1
  1.6 0.7 %copy-done.1 = s32[4,2,2,8]{3,2,1,0:T(2,128)S(1)} copy-done((s32[4,2,2,8]{3,2,1,0:T(2,128)S(1)}, s32[4,2,2,8]{3,2,1,0:T(2,128)}, u32[]{:S(2)}) %copy-start.1) | copy-done | bytes 536
  2.3 0.0 copy-start.2
  2.3 0.7 %copy-done.2 = f32[4,2,2,8]{3,2,1,0:T(2,128)S(1)} copy-done((f32[4,2,2,8]{3,2,1,0:T(2,128)S(1)}, f32[4,2,2,8]{3,2,1,0:T(2,128)}, u32[]{:S(2)}) %copy-start.2) | copy-done | bytes 536
  3.0 17.8 %shard_map.50 = f32[4,4,2,8,256]{4,3,2,1,0:T(8,128)S(1)} custom-call(f32[4,4,2,8,256]{4,3,2,1,0:T(8,128)S(1)} %copy-done, s32[4,2,2,8]{3,2,1,0:T(2,128)S(1)} %copy-done.1, f32[4,2,2,8]{3,2,1,0:T(2,128)S(1)} %copy-done.2), custom_call_target="tpu_custom_call" | custom-call | tf_op jit(solution)/shard_map/pallas_call | solution.py:374
  20.7 0.8 %multiply_subtract_fusion = (f32[4,4,2,8,256]{4,3,2,1,0:T(8,128)}, f32[4,4,2,8,256]{4,3,2,1,0:T(8,128)}) fusion(f32[4,4,2,8,256]{4,3,2,1,0:T(8,128)S(1)} %copy-done, f32[4,4,2,8,256]{4,3,2,1,0:T(8,128)S(1)} %shard_map.50), kind=kLoop, calls=%fused_computation | loop fusion | flops 196608 | bytes 1048576 | tf_op jit(solution)/shard_map/sub | solution.py:398
Async XLA Ops:
  0.6 1.0 %copy-start = (f32[4,4,2,8,256]{4,3,2,1,0:T(8,128)S(1)}, f32[4,4,2,8,256]{4,3,2,1,0:T(8,128)}, u32[]{:S(2)}) copy-start(f32[4,4,2,8,256]{4,3,2,1,0:T(8,128)} %state_in.1) | copy-start | bytes 786436
  1.6 0.7 %copy-start.1 = (s32[4,2,2,8]{3,2,1,0:T(2,128)S(1)}, s32[4,2,2,8]{3,2,1,0:T(2,128)}, u32[]{:S(2)}) copy-start(s32[4,2,2,8]{3,2,1,0:T(2,128)} %rows_in.1) | copy-start | bytes 1540
  2.3 0.7 %copy-start.2 = (f32[4,2,2,8]{3,2,1,0:T(2,128)S(1)}, f32[4,2,2,8]{3,2,1,0:T(2,128)}, u32[]{:S(2)}) copy-start(f32[4,2,2,8]{3,2,1,0:T(2,128)} %weights_in.1) | copy-start | bytes 1540

commit v2 on v1

--- a/solution.py
+++ b/solution.py
@@ -371,6 +371,10 @@
 
 def per_device(n, state, donor_rows, donor_weights):
     local, _, surfaces, rows, columns = state.shape
+    inputs = [
+        pltpu.with_memory_space_constraint(x, pltpu.HBM)
+        for x in (state, donor_rows, donor_weights)
+    ]
     half = pl.pallas_call(
         functools.partial(kernel, n, local, surfaces),
         out_shape=jax.ShapeDtypeStruct(state.shape, jnp.float32),
@@ -394,7 +398,7 @@
         compiler_params=pltpu.CompilerParams(
             collective_id=0, has_side_effects=True, vmem_limit_bytes=24 * 2**20
         ),
-    )(state, donor_rows, donor_weights)
+    )(*inputs)
     return state - (2.0 * time_step) * half, half + half
 
 

time: 21.8 us -> 19.4 us (0.89)
  local copies, waits for them, and re-layouts: 2.34 us -> 0.01 us
    unnamed x6 -> x2, local copies, waits for them, and re-layouts: 2.34 us -> 0.01 us
where the time goes in v2:
time: 19.4 us; the launch traced here: 19.3 us
  Pallas kernels  17.8 us (92%)
  other arithmetic  0.85 us (4%)
  between operations  0.65 us (3%)
    pallas_call x1, Pallas kernels, per_device(): pl.pallas_call(functools.partial(kernel, n, local, surfaces), out_shape=j...  17.8 us
    sub x1, other arithmetic, per_device(): return (state - 2.0 * time_step * half, half + half)  0.85 us

profile of v2, /device:TPU:0, one launch (start us, length us, event | category | flops | bytes accessed | tf_op | source)
XLA Modules:
  0.0 19.3 jit_solution(4183441629765941365)
XLA Ops:
  0.6 0.0 copy-start
  0.6 17.8 %shard_map.50 = f32[4,4,2,8,256]{4,3,2,1,0:T(8,128)S(1)} custom-call(f32[4,4,2,8,256]{4,3,2,1,0:T(8,128)} %state_in.1, s32[4,2,2,8]{3,2,1,0:T(2,128)} %rows_in.1, f32[4,2,2,8]{3,2,1,0:T(2,128)} %weights_in.1), custom_call_target="tpu_custom_call" | custom-call | tf_op jit(solution)/shard_map/pallas_call | solution.py:378
  18.4 0.0 copy-done
  18.4 0.8 %multiply_subtract_fusion = (f32[4,4,2,8,256]{4,3,2,1,0:T(8,128)}, f32[4,4,2,8,256]{4,3,2,1,0:T(8,128)}) fusion(f32[4,4,2,8,256]{4,3,2,1,0:T(8,128)S(1)} %copy-done, f32[4,4,2,8,256]{4,3,2,1,0:T(8,128)S(1)} %shard_map.50), kind=kLoop, calls=%fused_computation | loop fusion | flops 196608 | bytes 1048576 | tf_op jit(solution)/shard_map/sub | solution.py:402
Async XLA Ops:
  0.6 17.8 %copy-start = (f32[4,4,2,8,256]{4,3,2,1,0:T(8,128)S(1)}, f32[4,4,2,8,256]{4,3,2,1,0:T(8,128)}, u32[]{:S(2)}) copy-start(f32[4,4,2,8,256]{4,3,2,1,0:T(8,128)} %state_in.1) | copy-start | bytes 786436

commit v3 on v2

--- a/solution.py
+++ b/solution.py
@@ -105,21 +105,24 @@
         block = jnp.stack([state_ref[t, c, s] for t in range(local) for s in range(surfaces)])
         field[0, c, 2 : 2 + rows] = jnp.swapaxes(block, 0, 1)
 
-    loads[1].wait()
-    loads[2].wait()
     place = lane % 4
     lane_row = lane // 16
-    weight = []
-    for point in range(2):
-        total = jnp.zeros((8, LANES), jnp.float32)
-        for t in range(local):
-            for side in range(2):
-                mine = jnp.zeros((8, LANES), jnp.float32)
-                for r in range(rows):
-                    mine = jnp.where(lane_row == r, weights_ref[t, side, point, r], mine)
-                inside = (sub // surfaces == t) & ((place >= 2) if side == 0 else (place < 2))
-                total = jnp.where(inside, mine, total)
-        weight.append(total)
+
+    def donor_weights():
+        loads[1].wait()
+        loads[2].wait()
+        weight = []
+        for point in range(2):
+            total = jnp.zeros((8, LANES), jnp.float32)
+            for t in range(local):
+                for side in range(2):
+                    mine = jnp.zeros((8, LANES), jnp.float32)
+                    for r in range(rows):
+                        mine = jnp.where(lane_row == r, weights_ref[t, side, point, r], mine)
+                    inside = (sub // surfaces == t) & ((place >= 2) if side == 0 else (place < 2))
+                    total = jnp.where(inside, mine, total)
+            weight.append(total)
+        return weight
 
     def coefficients(offsets):
         out = jnp.zeros((8, 2 * LANES), jnp.float32)
@@ -136,17 +139,18 @@
 
     spot = lane % 16
 
-    def pack(section):
-        out = []
-        for c in range(4):
-            total = jnp.zeros((8, LANES), jnp.float32)
-            for r in range(rows):
+    def pack_rows(section, out, which):
+        for r in which:
+            for c in range(4):
                 rotor = field[section, c, 2 + r, :, 0:LANES]
                 stator = field[section, c, 2 + r, :, LANES : 2 * LANES]
-                edge = jnp.where(lane < 64, stator, rotor)
-                total = jnp.where(lane_row == r, lane_roll(edge, r * 16 + 3), total)
-            edges[section, c] = total
-            out.append(total)
+                edge = lane_roll(jnp.where(lane < 64, stator, rotor), r * 16 + 3)
+                out[c] = edge if out[c] is None else jnp.where(lane_row == r, edge, out[c])
+        return out
+
+    def pack_end(section, out):
+        for c in range(4):
+            edges[section, c] = out[c]
         total = lane_roll(out[0], -1)
         for c in range(1, 4):
             total = jnp.where(spot // 4 == c, lane_roll(out[c], c * 4 - 1), total)
@@ -190,7 +194,7 @@
             device_id={"inst": partner}, device_id_type=MESH,
         )
 
-    def interpolate(section):
+    def interpolate(section, weight):
         donors = [jnp.zeros((8, LANES), jnp.float32)] * 2
         for t in range(local):
             for side in range(2):
@@ -312,14 +316,27 @@
 
         lax.fori_loop(0, rows, one, 0, unroll=2)
 
-    def send(section):
-        top, bottom, cross = copies(section)
-        top.start()
-        bottom.start()
-        send_columns(section)
-        cross.start()
-
-    def together(section):
+        def inner(row, carry):
+            left, sense = carry
+            right, sense = circ_face(section, row + 2, sense)
+            for c in range(4):
+                acc[c, row] += right[c] - left[c]
+            return right, sense
+
+        zero = [jnp.zeros((8, 2 * LANES), jnp.float32)] * 4
+        left, _ = lax.fori_loop(1, rows - 2, inner, (zero, row_sensor(3)))
+        for c in range(4):
+            acc[c, rows - 2] -= left[c]
+
+    def finish(section, row, extra=None):
+        for c in range(4):
+            total = acc[c, row] if extra is None else acc[c, row] + extra[c]
+            if section == 0:
+                field[1, c, row + 2] = field[0, c, row + 2] - 0.5 * time_step * total
+            else:
+                acc[c, row] = 0.5 * total
+
+    def together(section, weight):
         top, bottom, cross = copies(section)
         cross.wait_recv()
 
@@ -330,34 +347,46 @@
 
         lax.fori_loop(0, rows, others, 0, unroll=2)
         all_columns(section).wait_recv()
-        interpolate(section)
+        interpolate(section, weight)
+        for row in range(2, rows - 2):
+            finish(section, row)
+        out = [None] * 4
+        if section == 0:
+            next_top, next_bottom, next_cross = copies(1)
+            out = pack_rows(1, out, range(2, rows - 2))
         top.wait_recv()
+        for row in (0, 1):
+            store_primitives(section, row)
+        first, sense = circ_face(section, 1, row_sensor(1))
+        second, _ = circ_face(section, 2, sense)
+        finish(section, 0, [second[c] - first[c] for c in range(4)])
+        finish(section, 1, [-second[c] for c in range(4)])
+        if section == 0:
+            out = pack_rows(1, out, (0, 1))
         bottom.wait_recv()
-        for row in (0, 1, rows + 2, rows + 3):
+        for row in (rows + 2, rows + 3):
             store_primitives(section, row)
-
-        def circ(row, carry):
-            left, sense = carry
-            right, sense = circ_face(section, row + 2, sense)
-            for c in range(4):
-                total = acc[c, row] + (right[c] - left[c])
-                if section == 0:
-                    field[1, c, row + 2] = field[0, c, row + 2] - 0.5 * time_step * total
-                else:
-                    acc[c, row] = 0.5 * total
-            return right, sense
-
-        lax.fori_loop(0, rows, circ, circ_face(section, 1, row_sensor(1)))
-
-    pack(0)
+        first, sense = circ_face(section, rows, row_sensor(rows))
+        second, _ = circ_face(section, rows + 1, sense)
+        finish(section, rows - 2, first)
+        finish(section, rows - 1, [second[c] - first[c] for c in range(4)])
+        if section == 0:
+            pack_end(1, pack_rows(1, out, (rows - 2, rows - 1)))
+            send_columns(1)
+            next_bottom.start()
+            next_top.start()
+            next_cross.start()
+
+    pack_end(0, pack_rows(0, [None] * 4, range(rows)))
+    pl.semaphore_wait(barrier, n)
+    send_columns(0)
+    for copy in copies(0):
+        copy.start()
+    weight = donor_weights()
     alone(0)
-    pl.semaphore_wait(barrier, n)
-    send(0)
-    together(0)
-    pack(1)
-    send(1)
+    together(0, weight)
     alone(1)
-    together(1)
+    together(1, weight)
     for c in range(4):
         block = jnp.swapaxes(acc[c], 0, 1)
         for t in range(local):

time: 19.4 us -> 18.1 us (0.933)
  Pallas kernels: 17.8 us -> 16.4 us
    pallas_call x1, Pallas kernels: 17.8 us -> 16.4 us  [per_device(): pl.pallas_call(functools.partial(kernel, n, local, surfaces), out_shape=j...]
where the time goes in v3:
time: 18.1 us; the launch traced here: 17.9 us
  Pallas kernels  16.4 us (91%)
  other arithmetic  0.85 us (5%)
  between operations  0.65 us (4%)
    pallas_call x1, Pallas kernels, per_device(): pl.pallas_call(functools.partial(kernel, n, local, surfaces), out_shape=j...  16.4 us
    sub x1, other arithmetic, per_device(): return (state - 2.0 * time_step * half, half + half)  0.85 us

profile of v3, /device:TPU:0, one launch (start us, length us, event | category | flops | bytes accessed | tf_op | source)
XLA Modules:
  0.0 17.9 jit_solution(2558526823714243139)
XLA Ops:
  0.6 0.0 copy-start
  0.6 16.4 %shard_map.50 = f32[4,4,2,8,256]{4,3,2,1,0:T(8,128)S(1)} custom-call(f32[4,4,2,8,256]{4,3,2,1,0:T(8,128)} %state_in.1, s32[4,2,2,8]{3,2,1,0:T(2,128)} %rows_in.1, f32[4,2,2,8]{3,2,1,0:T(2,128)} %weights_in.1), custom_call_target="tpu_custom_call" | custom-call | tf_op jit(solution)/shard_map/pallas_call | solution.py:407
  17.1 0.0 copy-done
  17.1 0.8 %multiply_subtract_fusion = (f32[4,4,2,8,256]{4,3,2,1,0:T(8,128)}, f32[4,4,2,8,256]{4,3,2,1,0:T(8,128)}) fusion(f32[4,4,2,8,256]{4,3,2,1,0:T(8,128)S(1)} %copy-done, f32[4,4,2,8,256]{4,3,2,1,0:T(8,128)S(1)} %shard_map.50), kind=kLoop, calls=%fused_computation | loop fusion | flops 196608 | bytes 1048576 | tf_op jit(solution)/shard_map/sub | solution.py:431
Async XLA Ops:
  0.6 16.4 %copy-start = (f32[4,4,2,8,256]{4,3,2,1,0:T(8,128)S(1)}, f32[4,4,2,8,256]{4,3,2,1,0:T(8,128)}, u32[]{:S(2)}) copy-start(f32[4,4,2,8,256]{4,3,2,1,0:T(8,128)} %state_in.1) | copy-start | bytes 786436

commit v4 on v3

--- a/solution.py
+++ b/solution.py
@@ -178,14 +178,18 @@
 
     def send_columns(section):
         def one(k, carry):
+            low = jnp.where(me < n // 2, 1, 0)
+            rank = low * (n - 1 - me) + (1 - low) * me
+            spot_k = k + jnp.where(k >= rank, 1, 0)
+            target = low * (n - 1 - spot_k) + (1 - low) * spot_k
             pltpu.make_async_remote_copy(
                 packed[section].at[me], packed[section].at[me],
                 send_sem.at[section, 3], recv_sem.at[section, 3],
-                device_id={"mesh": lax.rem(me + k, n)}, device_id_type=MESH,
+                device_id={"mesh": target}, device_id_type=MESH,
             ).start()
             return carry
 
-        lax.fori_loop(1, n, one, 0)
+        lax.fori_loop(0, n - 1, one, 0)
 
     def all_columns(section):
         return pltpu.make_async_remote_copy(
@@ -305,6 +309,21 @@
                 total = coef * value if total is None else total + coef * value
         return total
 
+    def start_halos(section):
+        top, bottom, cross = copies(section)
+
+        @pl.when(me < n // 2)
+        def _():
+            bottom.start()
+            top.start()
+
+        @pl.when(me >= n // 2)
+        def _():
+            top.start()
+            bottom.start()
+
+        cross.start()
+
     def alone(section):
         def one(row, carry):
             store_primitives(section, row + 2)
@@ -352,7 +371,6 @@
             finish(section, row)
         out = [None] * 4
         if section == 0:
-            next_top, next_bottom, next_cross = copies(1)
             out = pack_rows(1, out, range(2, rows - 2))
         top.wait_recv()
         for row in (0, 1):
@@ -373,15 +391,12 @@
         if section == 0:
             pack_end(1, pack_rows(1, out, (rows - 2, rows - 1)))
             send_columns(1)
-            next_bottom.start()
-            next_top.start()
-            next_cross.start()
+            start_halos(1)
 
     pack_end(0, pack_rows(0, [None] * 4, range(rows)))
     pl.semaphore_wait(barrier, n)
     send_columns(0)
-    for copy in copies(0):
-        copy.start()
+    start_halos(0)
     weight = donor_weights()
     alone(0)
     together(0, weight)

time: 18.1 us -> 18 us (level)
  no operation moved by 1% of the time
where the time goes in v4:
time: 18 us; the launch traced here: 17.8 us
  Pallas kernels  16.3 us (91%)
  other arithmetic  0.85 us (5%)
  between operations  0.65 us (4%)
    pallas_call x1, Pallas kernels, per_device(): pl.pallas_call(functools.partial(kernel, n, local, surfaces), out_shape=j...  16.3 us
    sub x1, other arithmetic, per_device(): return (state - 2.0 * time_step * half, half + half)  0.85 us

profile of v4, /device:TPU:0, one launch (start us, length us, event | category | flops | bytes accessed | tf_op | source)
XLA Modules:
  0.0 17.8 jit_solution(7513935674800789306)
XLA Ops:
  0.6 0.0 copy-start
  0.6 16.3 %shard_map.50 = f32[4,4,2,8,256]{4,3,2,1,0:T(8,128)S(1)} custom-call(f32[4,4,2,8,256]{4,3,2,1,0:T(8,128)} %state_in.1, s32[4,2,2,8]{3,2,1,0:T(2,128)} %rows_in.1, f32[4,2,2,8]{3,2,1,0:T(2,128)} %weights_in.1), custom_call_target="tpu_custom_call" | custom-call | tf_op jit(solution)/shard_map/pallas_call | solution.py:422
  16.9 0.0 copy-done
  17.0 0.8 %multiply_subtract_fusion = (f32[4,4,2,8,256]{4,3,2,1,0:T(8,128)}, f32[4,4,2,8,256]{4,3,2,1,0:T(8,128)}) fusion(f32[4,4,2,8,256]{4,3,2,1,0:T(8,128)S(1)} %copy-done, f32[4,4,2,8,256]{4,3,2,1,0:T(8,128)S(1)} %shard_map.50), kind=kLoop, calls=%fused_computation | loop fusion | flops 196608 | bytes 1048576 | tf_op jit(solution)/shard_map/sub | solution.py:446
Async XLA Ops:
  0.6 16.3 %copy-start = (f32[4,4,2,8,256]{4,3,2,1,0:T(8,128)S(1)}, f32[4,4,2,8,256]{4,3,2,1,0:T(8,128)}, u32[]{:S(2)}) copy-start(f32[4,4,2,8,256]{4,3,2,1,0:T(8,128)} %state_in.1) | copy-start | bytes 786436
